TPU v7x, 32 devices: a whole 2x2x4 slice. The times are simulated.
32 devices in a mesh: seq: 8 (over z, core), head: 4 (over y, x).
Axes of the slice: x: 2, y: 2, z: 4, core: 2. Of those that a mesh axis runs over, the one named last changes fastest.
Arguments:
- tokens: bfloat16 [512, 3072], P(('seq', 'head')), may hold values from -6 to 6
- w_qkv: bfloat16 [3, 3072, 3072], P(None, 'head'), may hold values from -0.109375 to 0.109375
- lr_weight: bfloat16 [48, 3072], P('head'), may hold values from -0.21875 to 0.21875
- lr_base: float32 [48], P('head'), may hold values from 0.3 to 3
- conv_weight: float32 [2, 4, 3072], P(None, None, 'head'), may hold values from -3 to 3
- w_init: float32 [2, 48, 64, 64], P(None, 'head'), may hold values from -0.75 to 0.75
- w_out: bfloat16 [3072, 3072], P('head'), may hold values from -0.15625 to 0.15625
Outputs:
- mixed: bfloat16 [512, 3072], P(('seq', 'head'))
All inputs are finite; a program needn't handle non-finite values.
Results may differ from a plain program's by a relative error of at most 0.018.
Values may be sent and summed in bfloat16 or wider, within the bound.
A program may use at most 128 MiB of HBM per device.

v0:
```python
import functools

import jax
import jax.numpy as jnp
from jax import lax
from jax.experimental import pallas as pl
from jax.experimental.pallas import tpu as pltpu
from jax.sharding import PartitionSpec as P

MB = 16
KERNEL = 4
EPSILON = 1e-05
LANES = 128
MESH = pl.DeviceIdType.MESH
F32, BF16 = jnp.float32, jnp.bfloat16


def mm(a, b):
    return jnp.dot(a, b, preferred_element_type=F32)


def layer(cfg, tok, wqkv, lrw, lrb, cw, winit, wout, out,
          xbuf, halo, xs, xt, wv, wov, lrwv, lrbv, cwv, wi, srate,
          maps, adds, wrecv, wsend, ht, pbuf, rbuf,
          lsem, wsem, tsend, trecv, hsend, hrecv, rsend, rrecv, psend, precv):
    n, nh, heads, hd, group, chunks = cfg
    own, depth = tok.shape
    rows = own * nh
    inner = heads * hd
    groups = heads // group
    g, me = lax.axis_index("seq"), lax.axis_index("head")
    not_first, not_last = g > 0, g < n - 1
    last_head = me == nh - 1

    small = [pltpu.make_async_copy(a, b, lsem.at[k]) for k, (a, b) in enumerate((
        (tok, xbuf.at[me]), (lrw, lrwv), (lrb, lrbv), (cw, cwv), (winit, wi)))]
    for copy in small:
        copy.start()
    weights = []
    for gi in range(groups):
        span = pl.ds(gi * group * hd, group * hd)
        weights.append([pltpu.make_async_copy(wqkv.at[c, span], wv.at[c, span], wsem.at[gi, c])
                        for c in range(3)])
        for copy in weights[-1]:
            copy.start()
    out_weight = pltpu.make_async_copy(wout, wov, lsem.at[5])
    out_weight.start()

    barrier = pltpu.get_barrier_semaphore()
    for i in range(1, nh):
        pl.semaphore_signal(barrier, inc=1, device_id=(g, lax.rem(me + i, nh)), device_id_type=MESH)

    @pl.when(not_first)
    def _():
        pl.semaphore_signal(barrier, inc=1, device_id=(g - 1, me), device_id_type=MESH)
        pl.semaphore_signal(barrier, inc=1, device_id=(g - 1, nh - 1), device_id_type=MESH)

    @pl.when(not_last)
    def _():
        pl.semaphore_signal(barrier, inc=1, device_id=(g + 1, me), device_id_type=MESH)

    pl.semaphore_wait(barrier, (nh - 1) + jnp.where(not_first, 1, 0) + jnp.where(not_last, 1, 0)
                      + jnp.where(last_head & not_last, nh, 0))

    def token_copy(i, slot):
        return pltpu.make_async_remote_copy(
            src_ref=tok, dst_ref=xbuf.at[slot], send_sem=tsend.at[i], recv_sem=trecv.at[i],
            device_id=(g, lax.rem(me + i, nh)), device_id_type=MESH)

    def halo_copy(h):
        return pltpu.make_async_remote_copy(
            src_ref=tok, dst_ref=halo, send_sem=hsend.at[h], recv_sem=hrecv.at[0],
            device_id=(g + 1, h), device_id_type=MESH)

    for i in range(1, nh):
        token_copy(i, me).start()

    @pl.when(last_head & not_last)
    def _():
        for h in range(nh):
            halo_copy(h).start()

    @pl.when(jnp.logical_not(not_first))
    def _():
        halo[...] = jnp.zeros_like(halo)

    xs[pl.ds(rows, LANES - own - rows), :] = jnp.zeros((LANES - own - rows, depth), F32)
    for copy in small:
        copy.wait()
    for i in range(1, nh):
        token_copy(i, lax.rem(me + nh - i, nh)).wait_recv()

    @pl.when(not_first)
    def _():
        halo_copy(0).wait_recv()

    for p in range(nh):
        xs[pl.ds(p * own, own), :] = xbuf[p].astype(F32)
    xs[pl.ds(LANES - own, own), :] = halo[...].astype(F32)
    for j in range(depth // LANES):
        cols = pl.ds(j * LANES, LANES)
        xt[cols, :] = xs[:, cols].T.astype(BF16)

    logit = mm(lrwv[...], xt[...])
    srate[...] = jnp.sqrt(lrbv[...] * jax.nn.sigmoid(logit) / MB)

    at_s = lax.broadcasted_iota(jnp.int32, (rows, rows), 0)
    at_t = lax.broadcasted_iota(jnp.int32, (rows, rows), 1)
    earlier = (at_s // MB) < (at_t // MB)
    causal, anti = at_s <= at_t, at_s >= at_t
    eye = (at_s == at_t).astype(F32)

    def convolved(gi, c):
        weights[gi][c].wait()
        span = pl.ds(gi * group * hd, group * hd)
        rounded = mm(wv[c, span, :], xt[...]).astype(BF16).astype(F32)
        if c == 2:
            return rounded
        taps = cwv[span, :]
        total = taps[:, c * KERNEL + KERNEL - 1:c * KERNEL + KERNEL] * rounded
        for p in range(KERNEL - 1):
            at = c * KERNEL + p
            total = total + taps[:, at:at + 1] * pltpu.roll(rounded, KERNEL - 1 - p, 1)
        return total

    for gi in range(groups):
        q_all, k_all, v_all = [convolved(gi, c) for c in range(3)]
        each = range(group)
        part = [slice(j * hd, (j + 1) * hd) for j in each]
        q = [q_all[s, :rows] for s in part]
        k = [k_all[s, :rows] for s in part]
        root = [srate[pl.ds(gi * group + j, 1), :][:, :rows] for j in each]
        k = [k[j] * (root[j] * lax.rsqrt(jnp.sum(k[j] * k[j], axis=0, keepdims=True)
                                         + EPSILON * hd)) for j in each]
        v = [(v_all[part[j], :rows] * root[j]).astype(BF16) for j in each]
        kt = [a.T.astype(BF16) for a in k]
        kb = [a.astype(BF16) for a in k]
        qb = [a.astype(BF16) for a in q]
        gram = [mm(kt[j], jnp.concatenate([kb[j], qb[j]], axis=1)) for j in each]
        one = [jnp.where(earlier, a[:, :rows], 0.0) for a in gram]
        oneb = [a.astype(BF16) for a in one]
        two = [mm(a, a) for a in oneb]
        three = [mm(oneb[j], two[j].astype(BF16)) for j in each]
        inv = [eye - one[j] + two[j] - three[j] for j in each]
        both = [jnp.concatenate([a, a.T], axis=1).astype(BF16) for a in inv]
        kv = [mm(jnp.concatenate([kb[j], v[j]], axis=0), both[j]) for j in each]
        for way, mask in ((0, causal), (1, anti)):
            left = [a[:, way * rows:(way + 1) * rows].astype(BF16) for a in kv]
            right = [jnp.concatenate(
                [kt[j], jnp.where(mask, gram[j][:, rows:], 0.0).astype(BF16)], axis=1) for j in each]
            made = [mm(left[j], right[j]) for j in each]
            for j in each:
                head = gi * group + j
                base = jnp.concatenate([jnp.zeros((hd, hd), F32), q[j]], axis=1)
                maps[way, head] = (base - made[j][:hd]).astype(BF16)
                adds[way, head] = made[j][hd:]

    def packed(a):
        return jnp.concatenate([a[:hd // 2], a[hd // 2:]], axis=1)

    def unpacked(a):
        return jnp.concatenate([a[:, :hd], a[:, hd:]], axis=0)

    @pl.when(jnp.logical_not(not_first))
    def _():
        for h in range(heads):
            wrecv[0, h] = packed(wi[0, h])

    @pl.when(jnp.logical_not(not_last))
    def _():
        for h in range(heads):
            wrecv[1, h] = packed(wi[1, h])

    def state_copy(way, gi):
        span = pl.ds(gi * group, group)
        return pltpu.make_async_remote_copy(
            src_ref=wsend.at[way, span], dst_ref=wrecv.at[way, span],
            send_sem=rsend.at[way, gi], recv_sem=rrecv.at[way, gi],
            device_id=(g + 1 - 2 * way, me), device_id_type=MESH)

    ways = []
    for d in range(2):
        way = jnp.where(g < n // 2, d, 1 - d)
        starts = jnp.where(way == 0, g, n - 1 - g) == 0
        ends = jnp.where(way == 0, n - 1 - g, g) == 0
        ways.append((way, ends))
        for gi in range(groups):
            @pl.when(jnp.logical_not(starts))
            def _():
                state_copy(way, gi).wait_recv()

            reach = []
            for j in range(group):
                head = gi * group + j
                state = unpacked(wrecv[way, head])
                new = mm(state.astype(BF16), maps[way, head]) + adds[way, head]
                wsend[way, head] = packed(state + new[:, :hd])
                reach.append(new[:, hd:])

            @pl.when(jnp.logical_not(ends))
            def _():
                state_copy(way, gi).start()

            for j in range(group):
                at = pl.ds((gi * group + j) * hd, hd)
                centred = reach[j] - jnp.mean(reach[j], axis=0, keepdims=True)
                spread = jnp.mean(centred * centred, axis=0, keepdims=True)
                normed = centred * lax.rsqrt(spread + EPSILON)
                if d == 0:
                    ht[at, pl.ds(0, rows)] = normed
                else:
                    ht[at, pl.ds(0, rows)] = ht[at, pl.ds(0, rows)] + normed

    hidden = jnp.concatenate(
        [ht[pl.ds(j * LANES, LANES), :].T[:rows] for j in range(ht.shape[0] // LANES)], axis=1)
    hidden = hidden[:, :inner].astype(BF16)
    out_weight.wait()

    def share_copy(j, i, to, slot):
        cols = pl.ds(j * (depth // chunks), depth // chunks)
        return pltpu.make_async_remote_copy(
            src_ref=pbuf.at[to, :, cols], dst_ref=rbuf.at[slot, :, cols],
            send_sem=psend.at[j, i], recv_sem=precv.at[j, i],
            device_id=(g, to), device_id_type=MESH)

    for j in range(chunks):
        cols = pl.ds(j * (depth // chunks), depth // chunks)
        share = mm(hidden, wov[:, cols])
        for p in range(nh):
            pbuf[p, :, cols] = share[p * own:(p + 1) * own].astype(BF16)
        for i in range(1, nh):
            share_copy(j, i, lax.rem(me + i, nh), me).start()

    for j in range(chunks):
        cols = pl.ds(j * (depth // chunks), depth // chunks)
        total = pbuf[me, :, cols].astype(F32)
        for i in range(1, nh):
            sender = lax.rem(me + nh - i, nh)
            share_copy(j, i, lax.rem(me + i, nh), sender).wait_recv()
            total = total + rbuf[sender, :, cols].astype(F32)
        out[:, cols] = total.astype(BF16)

    for i in range(1, nh):
        token_copy(i, me).wait_send()
        for j in range(chunks):
            share_copy(j, i, lax.rem(me + i, nh), me).wait_send()

    @pl.when(last_head & not_last)
    def _():
        for h in range(nh):
            halo_copy(h).wait_send()

    for way, ends in ways:
        @pl.when(jnp.logical_not(ends))
        def _():
            for gi in range(groups):
                state_copy(way, gi).wait_send()


def shards(n, nh, tokens, w_qkv, lr_weight, lr_base, conv_weight, w_init, w_out):
    own, depth = tokens.shape
    heads, hd = w_init.shape[1], w_init.shape[2]
    inner = heads * hd
    rows = own * nh
    group = max(k for k in (1, 2, 3, 4) if heads % k == 0)
    groups = heads // group
    chunks = 2
    padded = -(-inner // LANES) * LANES
    taps = jnp.transpose(conv_weight.reshape(2 * KERNEL, inner))
    any_space = pl.BlockSpec(memory_space=pl.ANY)
    dma = pltpu.SemaphoreType.DMA
    return pl.pallas_call(
        functools.partial(layer, (n, nh, heads, hd, group, chunks)),
        out_shape=jax.ShapeDtypeStruct((own, depth), BF16),
        in_specs=[any_space] * 7,
        out_specs=pl.BlockSpec(memory_space=pltpu.VMEM),
        scratch_shapes=[
            pltpu.VMEM((nh, own, depth), BF16),
            pltpu.VMEM((own, depth), BF16),
            pltpu.VMEM((LANES, depth), F32),
            pltpu.VMEM((depth, LANES), BF16),
            pltpu.VMEM(w_qkv.shape, BF16),
            pltpu.VMEM(w_out.shape, BF16),
            pltpu.VMEM(lr_weight.shape, BF16),
            pltpu.VMEM((heads, 1), F32),
            pltpu.VMEM((inner, 2 * KERNEL), F32),
            pltpu.VMEM(w_init.shape, F32),
            pltpu.VMEM((heads, LANES), F32),
            pltpu.VMEM((2, heads, hd, hd + rows), BF16),
            pltpu.VMEM((2, heads, hd, hd + rows), F32),
            pltpu.VMEM((2, heads, hd // 2, 2 * hd), F32),
            pltpu.VMEM((2, heads, hd // 2, 2 * hd), F32),
            pltpu.VMEM((padded, LANES), F32),
            pltpu.VMEM((nh, own, depth), BF16),
            pltpu.VMEM((nh, own, depth), BF16),
            dma((6,)),
            dma((groups, 3)),
            dma((nh,)),
            dma((nh,)),
            dma((nh,)),
            dma((1,)),
            dma((2, groups)),
            dma((2, groups)),
            dma((chunks, nh)),
            dma((chunks, nh)),
        ],
        compiler_params=pltpu.CompilerParams(
            collective_id=0, has_side_effects=True, vmem_limit_bytes=52 * 2 ** 20),
    )(tokens, w_qkv, lr_weight, lr_base.reshape(heads, 1), taps, w_init, w_out)


def solution(mesh):
    placed = (
        P(("seq", "head"), None),
        P(None, "head", None),
        P("head", None),
        P("head"),
        P(None, None, "head"),
        P(None, "head", None, None),
        P("head", None),
    )
    return jax.shard_map(
        functools.partial(shards, mesh.shape["seq"], mesh.shape["head"]),
        mesh=mesh, in_specs=placed, out_specs=P(("seq", "head"), None), check_vma=False
    )
```

profile of v0, /device:TPU:0, one launch (start us, length us, event | category | flops | bytes accessed | tf_op | source)
XLA Modules:
  0.0 50.0 jit_solution(2773924688536175364)
XLA Ops:
  0.0 0.7 %copy.11.lrb = f32[12,1]{1,0:T(8,128)S(1)} copy(f32[12,1]{0,1:T(1,128)} %bitcast.3) | data formatting | bytes 96 | tf_op jit(solution)/shard_map/reshape | solution.py:309
  0.7 0.7 %reshape.7 = f32[8,768]{1,0:T(8,128)S(1)} reshape(f32[2,4,768]{2,1,0:T(4,128)} %param.11) | data formatting | bytes 49152 | tf_op jit(solution)/shard_map/reshape | solution.py:269
  1.5 0.2 copy.10
  1.7 0.0 copy-start
  1.7 1.1 %copy-done = f32[2,12,64,64]{3,2,1,0:T(8,128)S(1)} copy-done((f32[2,12,64,64]{3,2,1,0:T(8,128)S(1)}, f32[2,12,64,64]{3,2,1,0:T(8,128)}, u32[]{:S(2)}) %copy-start) | copy-done | bytes 393240
  2.8 0.0 copy-start.1
  2.8 0.9 %copy-done.1 = bf16[16,3072]{1,0:T(8,128)(2,1)S(1)} copy-done((bf16[16,3072]{1,0:T(8,128)(2,1)S(1)}, bf16[16,3072]{1,0:T(8,128)(2,1)}, u32[]{:S(2)}) %copy-start.1) | copy-done | bytes 98328
  3.7 0.0 copy-start.2
  3.7 0.9 %copy-done.2 = bf16[12,3072]{1,0:T(8,128)(2,1)S(1)} copy-done((bf16[12,3072]{1,0:T(8,128)(2,1)S(1)}, bf16[12,3072]{1,0:T(8,128)(2,1)}, u32[]{:S(2)}) %copy-start.2) | copy-done | bytes 73752
  4.6 44.8 %shard_map.73 = bf16[16,3072]{1,0:T(8,128)(2,1)S(1)} custom-call(bf16[16,3072]{1,0:T(8,128)(2,1)S(1)} %copy-done.1, bf16[3,768,3072]{2,1,0:T(8,128)(2,1)} %wqkv.1, bf16[12,3072]{1,0:T(8,128)(2,1)S(1)} %copy-done.2, f32[12,1]{1,0:T(8,128)S(1)} %copy.11.lrb, f32[768,8]{1,0:T(8,128)S(1)} %bitcast.2, f32[2,12,64,64]{3,2,1,0:T(8,128)S(1)} %copy-done, ...), custom_call_target="tpu_custom_call" | custom-call | tf_op jit(solution)/shard_map/pallas_call | solution.py:272
  49.4 0.6 %copy.13 = bf16[16,3072]{1,0:T(8,128)(2,1)} copy(bf16[16,3072]{1,0:T(8,128)(2,1)S(1)} %shard_map.73) | data formatting | bytes 196608
Async XLA Ops:
  1.7 1.1 %copy-start = (f32[2,12,64,64]{3,2,1,0:T(8,128)S(1)}, f32[2,12,64,64]{3,2,1,0:T(8,128)}, u32[]{:S(2)}) copy-start(f32[2,12,64,64]{3,2,1,0:T(8,128)} %winit.1) | copy-start | bytes 1179652
  2.8 0.9 %copy-start.1 = (bf16[16,3072]{1,0:T(8,128)(2,1)S(1)}, bf16[16,3072]{1,0:T(8,128)(2,1)}, u32[]{:S(2)}) copy-start(bf16[16,3072]{1,0:T(8,128)(2,1)} %tok.1) | copy-start | bytes 294916
  3.7 0.9 %copy-start.2 = (bf16[12,3072]{1,0:T(8,128)(2,1)S(1)}, bf16[12,3072]{1,0:T(8,128)(2,1)}, u32[]{:S(2)}) copy-start(bf16[12,3072]{1,0:T(8,128)(2,1)} %lrw.1) | copy-start | bytes 221188
where the time goes:
time: 50.3 us; the launch traced here: 50 us
  Pallas kernels  44.8 us (89%)
  local copies, waits for them, and re-layouts  5.21 us (10%)
    pallas_call x1, Pallas kernels, shards(): pl.pallas_call(functools.partial(layer, (n, nh, heads, hd, group, chunks)...  44.8 us
    unnamed x7, local copies, waits for them, and re-layouts  3.56 us

commit v1 on v0

v1 whole, which is shorter than its diff:
```python
import functools

import jax
import jax.numpy as jnp
from jax import lax
from jax.experimental import pallas as pl
from jax.experimental.pallas import tpu as pltpu
from jax.sharding import PartitionSpec as P

MB = 16
KERNEL = 4
EPSILON = 1e-05
LANES = 128
MESH = pl.DeviceIdType.MESH
F32, BF16 = jnp.float32, jnp.bfloat16


def mm(a, b):
    return jnp.dot(a, b, preferred_element_type=F32)


def layer(cfg, tok, wqkv, lrw, lrb, cw, winit, wout, out,
          xbuf, halo, xs, xt, wv, wov, lrwv, cwv, cwt, taps_ref, wi, gate,
          maps, adds, states, sending, reach, kept, pbuf, rbuf,
          lsem, wsem, tsend, trecv, hsend, hrecv, rsend, rrecv, psend, precv):
    n, nh, heads, hd, pair_group, chunks = cfg
    own, depth = tok.shape
    rows = own * nh
    inner = heads * hd
    pairs = (heads + 1) // 2
    groups = pairs // pair_group
    wide = 2 * hd
    g, me = lax.axis_index("seq"), lax.axis_index("head")
    not_first, not_last = g > 0, g < n - 1
    last_head = me == nh - 1

    small = [pltpu.make_async_copy(a, b, lsem.at[k]) for k, (a, b) in enumerate((
        (tok, xbuf.at[me]), (lrw, lrwv), (cw, cwv), (winit, wi)))]
    for copy in small:
        copy.start()
    weights = []
    for gi in range(groups):
        start = gi * pair_group * wide
        span = pl.ds(start, min(pair_group * wide, inner - start))
        weights.append([pltpu.make_async_copy(wqkv.at[c, span], wv.at[c, span], wsem.at[gi, c])
                        for c in range(3)])
        for copy in weights[-1]:
            copy.start()
    out_weight = pltpu.make_async_copy(wout, wov, lsem.at[4])
    out_weight.start()

    barrier = pltpu.get_barrier_semaphore()
    for i in range(1, nh):
        pl.semaphore_signal(barrier, inc=1, device_id=(g, lax.rem(me + i, nh)), device_id_type=MESH)

    @pl.when(not_first)
    def _():
        pl.semaphore_signal(barrier, inc=1, device_id=(g - 1, me), device_id_type=MESH)
        pl.semaphore_signal(barrier, inc=1, device_id=(g - 1, nh - 1), device_id_type=MESH)

    @pl.when(not_last)
    def _():
        pl.semaphore_signal(barrier, inc=1, device_id=(g + 1, me), device_id_type=MESH)

    pl.semaphore_wait(barrier, (nh - 1) + jnp.where(not_first, 1, 0) + jnp.where(not_last, 1, 0)
                      + jnp.where(last_head & not_last, nh, 0))

    def token_copy(i, slot):
        return pltpu.make_async_remote_copy(
            src_ref=tok, dst_ref=xbuf.at[slot], send_sem=tsend.at[i], recv_sem=trecv.at[i],
            device_id=(g, lax.rem(me + i, nh)), device_id_type=MESH)

    def halo_copy(h):
        return pltpu.make_async_remote_copy(
            src_ref=tok, dst_ref=halo, send_sem=hsend.at[h], recv_sem=hrecv.at[0],
            device_id=(g + 1, h), device_id_type=MESH)

    for i in range(1, nh):
        token_copy(i, me).start()

    @pl.when(last_head & not_last)
    def _():
        for h in range(nh):
            halo_copy(h).start()

    @pl.when(jnp.logical_not(not_first))
    def _():
        halo[...] = jnp.zeros_like(halo)

    xs[pl.ds(rows, LANES - own - rows), :] = jnp.zeros((LANES - own - rows, depth), F32)
    for copy in small:
        copy.wait()

    cwt[...] = jnp.zeros_like(cwt)
    for c in range(2):
        cwt[pl.ds(c * KERNEL, KERNEL), pl.ds(0, inner)] = cwv[c]
    for j in range(pairs):
        taps_ref[pl.ds(j * LANES, LANES), :] = cwt[:, pl.ds(j * LANES, LANES)].T

    for way, outer in ((0, jnp.logical_not(not_first)), (1, jnp.logical_not(not_last))):
        @pl.when(outer)
        def _():
            for p in range(pairs):
                second = wi[way, 2 * p + 1] if 2 * p + 1 < heads else jnp.zeros((hd, hd), F32)
                states[way, p] = jnp.concatenate([wi[way, 2 * p], second], axis=1).astype(BF16)

    for i in range(1, nh):
        token_copy(i, lax.rem(me + nh - i, nh)).wait_recv()

    @pl.when(not_first)
    def _():
        halo_copy(0).wait_recv()

    for p in range(nh):
        xs[pl.ds(p * own, own), :] = xbuf[p].astype(F32)
    xs[pl.ds(LANES - own, own), :] = halo[...].astype(F32)
    for j in range(depth // LANES):
        cols = pl.ds(j * LANES, LANES)
        xt[cols, :] = xs[:, cols].T.astype(BF16)

    gate[...] = jax.nn.sigmoid(mm(lrwv[...], xt[...]))

    at_s = lax.broadcasted_iota(jnp.int32, (wide, wide), 0)
    at_t = lax.broadcasted_iota(jnp.int32, (wide, wide), 1)
    upper, left_half = at_s < hd, at_t < rows
    same = upper == left_half
    earlier = same & ((at_s // MB) < (at_t // MB))
    causal, anti = same & (at_s <= at_t), same & (at_s >= at_t)
    eye = (at_s == at_t).astype(F32)
    row_left = left_half[:1]

    def diagonal(a):
        return jnp.where(same, jnp.where(upper, a, pltpu.roll(a, rows, 1)), 0.0)

    def root_rate(p):
        first = gate[pl.ds(2 * p, 1), :] * lrb[2 * p]
        if 2 * p + 1 == heads:
            return jnp.sqrt(jnp.where(row_left, first, 0.0) / MB)
        second = gate[pl.ds(2 * p + 1, 1), :] * lrb[2 * p + 1]
        return jnp.sqrt(jnp.where(row_left, first, pltpu.roll(second, rows, 1)) / MB)

    def convolved(gi, c):
        weights[gi][c].wait()
        span = pl.ds(gi * pair_group * wide, pair_group * wide)
        rounded = mm(wv[c, span, :], xt[...]).astype(BF16).astype(F32)
        if inner < pairs * wide:
            row = lax.broadcasted_iota(jnp.int32, rounded.shape, 0) + gi * pair_group * wide
            rounded = jnp.where(row < inner, rounded, 0.0)
        if c == 2:
            return rounded
        taps = taps_ref[span, :]
        total = taps[:, c * KERNEL + KERNEL - 1:c * KERNEL + KERNEL] * rounded
        for p in range(KERNEL - 1):
            at = c * KERNEL + p
            total = total + taps[:, at:at + 1] * pltpu.roll(rounded, KERNEL - 1 - p, 1)
        return total

    for gi in range(groups):
        q_all, k_all, v_all = [convolved(gi, c) for c in range(3)]
        each = range(pair_group)
        part = [slice(j * wide, (j + 1) * wide) for j in each]
        root = [root_rate(gi * pair_group + j) for j in each]
        q = [diagonal(q_all[s]) for s in part]
        k = [diagonal(k_all[s]) for s in part]
        k = [k[j] * (root[j] * lax.rsqrt(jnp.sum(k[j] * k[j], axis=0, keepdims=True)
                                         + EPSILON * hd)) for j in each]
        v = [(diagonal(v_all[part[j]]) * root[j]).astype(BF16) for j in each]
        kt = [a.T.astype(BF16) for a in k]
        kb = [a.astype(BF16) for a in k]
        qb = [a.astype(BF16) for a in q]
        gram = [mm(kt[j], jnp.concatenate([kb[j], qb[j]], axis=1)) for j in each]
        one = [jnp.where(earlier, a[:, :wide], 0.0) for a in gram]
        oneb = [a.astype(BF16) for a in one]
        two = [mm(a, a) for a in oneb]
        three = [mm(oneb[j], two[j].astype(BF16)) for j in each]
        inv = [eye - one[j] + two[j] - three[j] for j in each]
        both = [jnp.concatenate([a, a.T], axis=1).astype(BF16) for a in inv]
        kv = [mm(jnp.concatenate([kb[j], v[j]], axis=0), both[j]) for j in each]
        for way, mask in ((0, causal), (1, anti)):
            lhs = [a[:, way * wide:(way + 1) * wide].astype(BF16) for a in kv]
            rhs = [jnp.concatenate(
                [kt[j], jnp.where(mask, gram[j][:, wide:], 0.0).astype(BF16)], axis=1) for j in each]
            made = [mm(lhs[j], rhs[j]) for j in each]
            for j in each:
                p = gi * pair_group + j
                maps[way, p, :, pl.ds(0, wide)] = (-made[j][:wide, :wide]).astype(BF16)
                maps[way, p, :, pl.ds(wide, wide)] = (q[j] - made[j][:wide, wide:]).astype(BF16)
                adds[way, p] = made[j][wide:wide + hd] + made[j][wide + hd:]

    def state_copy(way, gi):
        span = pl.ds(gi * pair_group, pair_group)
        return pltpu.make_async_remote_copy(
            src_ref=sending.at[way, span], dst_ref=states.at[way, span],
            send_sem=rsend.at[way, gi], recv_sem=rrecv.at[way, gi],
            device_id=(g + 1 - 2 * way, me), device_id_type=MESH)

    ways, normed = [], []
    for d in range(2):
        way = jnp.where(g < n // 2, d, 1 - d)
        starts = jnp.where(way == 0, g, n - 1 - g) == 0
        ends = jnp.where(way == 0, n - 1 - g, g) == 0
        ways.append((way, ends))
        for gi in range(groups):
            @pl.when(jnp.logical_not(starts))
            def _():
                state_copy(way, gi).wait_recv()

            mine = range(gi * pair_group, (gi + 1) * pair_group)
            old = [states[way, p] for p in mine]
            new = [mm(a, maps[way, p]) + adds[way, p] for a, p in zip(old, mine)]
            for a, b, p in zip(old, new, mine):
                sending[way, p] = (a.astype(F32) + b[:, :wide]).astype(BF16)

            @pl.when(jnp.logical_not(ends))
            def _():
                state_copy(way, gi).start()

            for b, p in zip(new, mine):
                reach[p] = b[:, wide:]

        for p in range(pairs):
            got = reach[p]
            centred = got - jnp.mean(got, axis=0, keepdims=True)
            spread = jnp.mean(centred * centred, axis=0, keepdims=True)
            scaled = centred * lax.rsqrt(spread + EPSILON)
            if d == 0:
                kept[p] = scaled
            else:
                normed.append(scaled + kept[p])

    turned = [a.T for a in normed]
    hidden = jnp.concatenate(
        [jnp.concatenate([a[:rows], a[rows:]], axis=1) for a in turned], axis=1)
    hidden = hidden[:, :inner].astype(BF16)
    out_weight.wait()

    def share_copy(j, i, to, slot):
        cols = pl.ds(j * (depth // chunks), depth // chunks)
        return pltpu.make_async_remote_copy(
            src_ref=pbuf.at[to, :, cols], dst_ref=rbuf.at[slot, :, cols],
            send_sem=psend.at[j, i], recv_sem=precv.at[j, i],
            device_id=(g, to), device_id_type=MESH)

    for j in range(chunks):
        cols = pl.ds(j * (depth // chunks), depth // chunks)
        share = mm(hidden, wov[:, cols])
        for p in range(nh):
            pbuf[p, :, cols] = share[p * own:(p + 1) * own].astype(BF16)
        for i in range(1, nh):
            share_copy(j, i, lax.rem(me + i, nh), me).start()

    for j in range(chunks):
        cols = pl.ds(j * (depth // chunks), depth // chunks)
        total = pbuf[me, :, cols].astype(F32)
        for i in range(1, nh):
            sender = lax.rem(me + nh - i, nh)
            share_copy(j, i, lax.rem(me + i, nh), sender).wait_recv()
            total = total + rbuf[sender, :, cols].astype(F32)
        out[:, cols] = total.astype(BF16)

    for i in range(1, nh):
        token_copy(i, me).wait_send()
        for j in range(chunks):
            share_copy(j, i, lax.rem(me + i, nh), me).wait_send()

    @pl.when(last_head & not_last)
    def _():
        for h in range(nh):
            halo_copy(h).wait_send()

    for way, ends in ways:
        @pl.when(jnp.logical_not(ends))
        def _():
            for gi in range(groups):
                state_copy(way, gi).wait_send()


def shards(n, nh, tokens, w_qkv, lr_weight, lr_base, conv_weight, w_init, w_out):
    own, depth = tokens.shape
    heads, hd = w_init.shape[1], w_init.shape[2]
    inner = heads * hd
    pairs = (heads + 1) // 2
    padded = pairs * 2 * hd
    pair_group = 2 if pairs % 2 == 0 else 1
    groups = pairs // pair_group
    chunks = 2
    wide = 2 * hd
    hbm = pl.BlockSpec(memory_space=pltpu.HBM)
    smem = pl.BlockSpec(memory_space=pltpu.SMEM)
    dma = pltpu.SemaphoreType.DMA
    return pl.pallas_call(
        functools.partial(layer, (n, nh, heads, hd, pair_group, chunks)),
        out_shape=jax.ShapeDtypeStruct((own, depth), BF16),
        in_specs=[hbm, hbm, hbm, smem, hbm, hbm, hbm],
        out_specs=pl.BlockSpec(memory_space=pltpu.VMEM),
        scratch_shapes=[
            pltpu.VMEM((nh, own, depth), BF16),
            pltpu.VMEM((own, depth), BF16),
            pltpu.VMEM((LANES, depth), F32),
            pltpu.VMEM((depth, LANES), BF16),
            pltpu.VMEM((3, padded, depth), BF16),
            pltpu.VMEM(w_out.shape, BF16),
            pltpu.VMEM(lr_weight.shape, BF16),
            pltpu.VMEM(conv_weight.shape, F32),
            pltpu.VMEM((LANES, padded), F32),
            pltpu.VMEM((padded, LANES), F32),
            pltpu.VMEM(w_init.shape, F32),
            pltpu.VMEM((heads, LANES), F32),
            pltpu.VMEM((2, pairs, wide, 2 * wide), BF16),
            pltpu.VMEM((2, pairs, hd, 2 * wide), F32),
            pltpu.VMEM((2, pairs, hd, wide), BF16),
            pltpu.VMEM((2, pairs, hd, wide), BF16),
            pltpu.VMEM((pairs, hd, wide), F32),
            pltpu.VMEM((pairs, hd, wide), F32),
            pltpu.VMEM((nh, own, depth), BF16),
            pltpu.VMEM((nh, own, depth), BF16),
            dma((5,)),
            dma((groups, 3)),
            dma((nh,)),
            dma((nh,)),
            dma((nh,)),
            dma((1,)),
            dma((2, groups)),
            dma((2, groups)),
            dma((chunks, nh)),
            dma((chunks, nh)),
        ],
        compiler_params=pltpu.CompilerParams(
            collective_id=0, has_side_effects=True, vmem_limit_bytes=60 * 2 ** 20),
    )(tokens, w_qkv, lr_weight, lr_base, conv_weight, w_init, w_out)


def solution(mesh):
    placed = (
        P(("seq", "head"), None),
        P(None, "head", None),
        P("head", None),
        P("head"),
        P(None, None, "head"),
        P(None, "head", None, None),
        P("head", None),
    )
    return jax.shard_map(
        functools.partial(shards, mesh.shape["seq"], mesh.shape["head"]),
        mesh=mesh, in_specs=placed, out_specs=P(("seq", "head"), None), check_vma=False
    )
```

time: 50.3 us -> 44.6 us (0.89)
  local copies, waits for them, and re-layouts: 5.21 us -> 1.54 us
  Pallas kernels: 44.8 us -> 42.7 us
    pallas_call x1, Pallas kernels: 44.8 us -> 42.7 us  [shards(): pl.pallas_call(functools.partial(layer, (n, nh, heads, hd, pair_group, ch...]
    unnamed x7 -> x1, local copies, waits for them, and re-layouts: 3.56 us -> 1.54 us
    reshape x3 -> x0, local copies, waits for them, and re-layouts: 1.65 us -> none  [the longest x2 0.91 us: shards(): taps = jnp.transpose(conv_weight.reshape(2 * KERNEL, inner))]
where the time goes in v1:
time: 44.6 us; the launch traced here: 44.3 us
  Pallas kernels  42.7 us (96%)
  local copies, waits for them, and re-layouts  1.54 us (3%)
    pallas_call x1, Pallas kernels, shards(): pl.pallas_call(functools.partial(layer, (n, nh, heads, hd, pair_group, ch...  42.7 us
    unnamed x1, local copies, waits for them, and re-layouts  1.54 us

profile of v1, /device:TPU:0, one launch (start us, length us, event | category | flops | bytes accessed | tf_op | source)
XLA Modules:
  0.0 44.3 jit_solution(12808378840605922397)
XLA Ops:
  0.0 42.7 %shard_map.73 = bf16[16,3072]{1,0:T(8,128)(2,1)} custom-call(bf16[16,3072]{1,0:T(8,128)(2,1)} %tok.1, bf16[3,768,3072]{2,1,0:T(8,128)(2,1)} %wqkv.1, bf16[12,3072]{1,0:T(8,128)(2,1)} %lrw.1, f32[12]{0:T(128)} %lrb.1, f32[2,4,768]{2,1,0:T(4,128)} %cw.1, f32[2,12,64,64]{3,2,1,0:T(8,128)} %winit.1, bf16[768,3072]{1,0:T(8,128)(2,1)} %wout.1), custom_call_target="tpu_custom_call" | custom-call | tf_op jit(solution)/shard_map/pallas_call | solution.py:291
  42.7 1.5 %copy.9 = bf16[16,3072]{1,0:T(8,128)(2,1)} copy(bf16[16,3072]{1,0:T(8,128)(2,1)} %shard_map.73) | data formatting | bytes 196608

commit v2 on v1

--- a/solution.py
+++ b/solution.py
@@ -19,8 +19,12 @@
     return jnp.dot(a, b, preferred_element_type=F32)
 
 
+def mm_rows(a, b):
+    return lax.dot_general(a, b, (((1,), (1,)), ((), ())), preferred_element_type=F32)
+
+
 def layer(cfg, tok, wqkv, lrw, lrb, cw, winit, wout, out,
-          xbuf, halo, xs, xt, wv, wov, lrwv, cwv, cwt, taps_ref, wi, gate,
+          xbuf, rim, halo, xs, xt, wv, wov, lrwv, cwv, cwt, taps_ref, wi, gate,
           maps, adds, states, sending, reach, kept, pbuf, rbuf,
           lsem, wsem, tsend, trecv, hsend, hrecv, rsend, rrecv, psend, precv):
     n, nh, heads, hd, pair_group, chunks = cfg
@@ -39,13 +43,9 @@
     for copy in small:
         copy.start()
     weights = []
-    for gi in range(groups):
-        start = gi * pair_group * wide
-        span = pl.ds(start, min(pair_group * wide, inner - start))
-        weights.append([pltpu.make_async_copy(wqkv.at[c, span], wv.at[c, span], wsem.at[gi, c])
-                        for c in range(3)])
-        for copy in weights[-1]:
-            copy.start()
+    for c in range(3):
+        weights.append(pltpu.make_async_copy(wqkv.at[c], wv.at[c, pl.ds(0, inner)], wsem.at[c]))
+        weights[c].start()
     out_weight = pltpu.make_async_copy(wout, wov, lsem.at[4])
     out_weight.start()
 
@@ -72,12 +72,20 @@
 
     def halo_copy(h):
         return pltpu.make_async_remote_copy(
-            src_ref=tok, dst_ref=halo, send_sem=hsend.at[h], recv_sem=hrecv.at[0],
+            src_ref=rim, dst_ref=halo, send_sem=hsend.at[h], recv_sem=hrecv.at[0],
             device_id=(g + 1, h), device_id_type=MESH)
 
     for i in range(1, nh):
         token_copy(i, me).start()
 
+    small[0].wait()
+    rim_rows = KERNEL - 1
+    piece = depth // rim_rows
+    mine_last = xbuf[me].astype(F32)[own - rim_rows:]
+    rim[...] = jnp.concatenate(
+        [mine_last[r:r + 1, c * piece:(c + 1) * piece] for r in range(rim_rows) for c in range(rim_rows)]
+        + [jnp.zeros((rim.shape[0] - rim_rows * rim_rows, piece), F32)], axis=0).astype(BF16)
+
     @pl.when(last_head & not_last)
     def _():
         for h in range(nh):
@@ -87,8 +95,7 @@
     def _():
         halo[...] = jnp.zeros_like(halo)
 
-    xs[pl.ds(rows, LANES - own - rows), :] = jnp.zeros((LANES - own - rows, depth), F32)
-    for copy in small:
+    for copy in small[1:]:
         copy.wait()
 
     cwt[...] = jnp.zeros_like(cwt)
@@ -111,14 +118,21 @@
     def _():
         halo_copy(0).wait_recv()
 
-    for p in range(nh):
-        xs[pl.ds(p * own, own), :] = xbuf[p].astype(F32)
-    xs[pl.ds(LANES - own, own), :] = halo[...].astype(F32)
-    for j in range(depth // LANES):
-        cols = pl.ds(j * LANES, LANES)
-        xt[cols, :] = xs[:, cols].T.astype(BF16)
-
-    gate[...] = jax.nn.sigmoid(mm(lrwv[...], xt[...]))
+    tail = halo[...].astype(F32)
+    tail = [jnp.concatenate([tail[r * rim_rows + c:r * rim_rows + c + 1] for c in range(rim_rows)], axis=1)
+            for r in range(rim_rows)]
+    tail = jnp.concatenate([jnp.zeros((16 - rim_rows, depth), F32)] + tail, axis=0)
+    if own % 16 == 0:
+        for p in range(nh):
+            xt[pl.ds(p * own, own), :] = xbuf[p]
+    else:
+        for p in range(nh):
+            xs[pl.ds(p * own, own), :] = xbuf[p].astype(F32)
+        xt[pl.ds(0, rows), :] = xs[pl.ds(0, rows), :].astype(BF16)
+    xt[pl.ds(rows, LANES - 16 - rows), :] = jnp.zeros((LANES - 16 - rows, depth), BF16)
+    xt[pl.ds(LANES - 16, 16), :] = tail.astype(BF16)
+
+    gate[...] = jax.nn.sigmoid(mm_rows(lrwv[...], xt[...]))
 
     at_s = lax.broadcasted_iota(jnp.int32, (wide, wide), 0)
     at_t = lax.broadcasted_iota(jnp.int32, (wide, wide), 1)
@@ -139,53 +153,51 @@
         second = gate[pl.ds(2 * p + 1, 1), :] * lrb[2 * p + 1]
         return jnp.sqrt(jnp.where(row_left, first, pltpu.roll(second, rows, 1)) / MB)
 
-    def convolved(gi, c):
-        weights[gi][c].wait()
-        span = pl.ds(gi * pair_group * wide, pair_group * wide)
-        rounded = mm(wv[c, span, :], xt[...]).astype(BF16).astype(F32)
+    def convolved(c):
+        weights[c].wait()
+        rounded = mm_rows(wv[c], xt[...]).astype(BF16).astype(F32)
         if inner < pairs * wide:
-            row = lax.broadcasted_iota(jnp.int32, rounded.shape, 0) + gi * pair_group * wide
+            row = lax.broadcasted_iota(jnp.int32, rounded.shape, 0)
             rounded = jnp.where(row < inner, rounded, 0.0)
         if c == 2:
             return rounded
-        taps = taps_ref[span, :]
+        taps = taps_ref[...]
         total = taps[:, c * KERNEL + KERNEL - 1:c * KERNEL + KERNEL] * rounded
         for p in range(KERNEL - 1):
             at = c * KERNEL + p
             total = total + taps[:, at:at + 1] * pltpu.roll(rounded, KERNEL - 1 - p, 1)
         return total
 
-    for gi in range(groups):
-        q_all, k_all, v_all = [convolved(gi, c) for c in range(3)]
-        each = range(pair_group)
-        part = [slice(j * wide, (j + 1) * wide) for j in each]
-        root = [root_rate(gi * pair_group + j) for j in each]
-        q = [diagonal(q_all[s]) for s in part]
-        k = [diagonal(k_all[s]) for s in part]
-        k = [k[j] * (root[j] * lax.rsqrt(jnp.sum(k[j] * k[j], axis=0, keepdims=True)
-                                         + EPSILON * hd)) for j in each]
-        v = [(diagonal(v_all[part[j]]) * root[j]).astype(BF16) for j in each]
-        kt = [a.T.astype(BF16) for a in k]
-        kb = [a.astype(BF16) for a in k]
-        qb = [a.astype(BF16) for a in q]
-        gram = [mm(kt[j], jnp.concatenate([kb[j], qb[j]], axis=1)) for j in each]
-        one = [jnp.where(earlier, a[:, :wide], 0.0) for a in gram]
-        oneb = [a.astype(BF16) for a in one]
-        two = [mm(a, a) for a in oneb]
-        three = [mm(oneb[j], two[j].astype(BF16)) for j in each]
-        inv = [eye - one[j] + two[j] - three[j] for j in each]
-        both = [jnp.concatenate([a, a.T], axis=1).astype(BF16) for a in inv]
-        kv = [mm(jnp.concatenate([kb[j], v[j]], axis=0), both[j]) for j in each]
-        for way, mask in ((0, causal), (1, anti)):
-            lhs = [a[:, way * wide:(way + 1) * wide].astype(BF16) for a in kv]
-            rhs = [jnp.concatenate(
-                [kt[j], jnp.where(mask, gram[j][:, wide:], 0.0).astype(BF16)], axis=1) for j in each]
-            made = [mm(lhs[j], rhs[j]) for j in each]
-            for j in each:
-                p = gi * pair_group + j
-                maps[way, p, :, pl.ds(0, wide)] = (-made[j][:wide, :wide]).astype(BF16)
-                maps[way, p, :, pl.ds(wide, wide)] = (q[j] - made[j][:wide, wide:]).astype(BF16)
-                adds[way, p] = made[j][wide:wide + hd] + made[j][wide + hd:]
+    q_all, k_all, v_all = [convolved(c) for c in range(3)]
+    each = range(pairs)
+    part = [slice(j * wide, (j + 1) * wide) for j in each]
+    root = [root_rate(j) for j in each]
+    q = [diagonal(q_all[s]) for s in part]
+    k = [diagonal(k_all[s]) for s in part]
+    k = [k[j] * (root[j] * lax.rsqrt(jnp.sum(k[j] * k[j], axis=0, keepdims=True)
+                                     + EPSILON * hd)) for j in each]
+    v = [(diagonal(v_all[part[j]]) * root[j]).astype(BF16) for j in each]
+    kt = [a.T.astype(BF16) for a in k]
+    kb = [a.astype(BF16) for a in k]
+    qb = [a.astype(BF16) for a in q]
+    gram = [mm(kt[j], jnp.concatenate([kb[j], qb[j]], axis=1)) for j in each]
+    one = [jnp.where(earlier, a[:, :wide], 0.0) for a in gram]
+    oneb = [a.astype(BF16) for a in one]
+    two = [mm(a, a) for a in oneb]
+    three = [mm(oneb[j], two[j].astype(BF16)) for j in each]
+    inv = [eye - one[j] + two[j] - three[j] for j in each]
+    both = [jnp.concatenate([a, a.T], axis=1).astype(BF16) for a in inv]
+    kv = [mm(jnp.concatenate([kb[j], v[j]], axis=0), both[j]) for j in each]
+    for way, mask in ((0, causal), (1, anti)):
+        lhs = [a[:, way * wide:(way + 1) * wide].astype(BF16) for a in kv]
+        rhs = [jnp.concatenate(
+            [kt[j], jnp.where(mask, gram[j][:, wide:], 0.0).astype(BF16)], axis=1) for j in each]
+        made = [mm(lhs[j], rhs[j]) for j in each]
+        for j in each:
+            p = j
+            maps[way, p, :, pl.ds(0, wide)] = (-made[j][:wide, :wide]).astype(BF16)
+            maps[way, p, :, pl.ds(wide, wide)] = (q[j] - made[j][:wide, wide:]).astype(BF16)
+            adds[way, p] = made[j][wide:wide + hd] + made[j][wide + hd:]
 
     def state_copy(way, gi):
         span = pl.ds(gi * pair_group, pair_group)
@@ -279,6 +291,7 @@
     own, depth = tokens.shape
     heads, hd = w_init.shape[1], w_init.shape[2]
     inner = heads * hd
+    rows = own * nh
     pairs = (heads + 1) // 2
     padded = pairs * 2 * hd
     pair_group = 2 if pairs % 2 == 0 else 1
@@ -295,9 +308,10 @@
         out_specs=pl.BlockSpec(memory_space=pltpu.VMEM),
         scratch_shapes=[
             pltpu.VMEM((nh, own, depth), BF16),
-            pltpu.VMEM((own, depth), BF16),
-            pltpu.VMEM((LANES, depth), F32),
-            pltpu.VMEM((depth, LANES), BF16),
+            pltpu.VMEM((16, depth // (KERNEL - 1)), BF16),
+            pltpu.VMEM((16, depth // (KERNEL - 1)), BF16),
+            pltpu.VMEM((rows, depth) if own % 16 else (8, LANES), F32),
+            pltpu.VMEM((LANES, depth), BF16),
             pltpu.VMEM((3, padded, depth), BF16),
             pltpu.VMEM(w_out.shape, BF16),
             pltpu.VMEM(lr_weight.shape, BF16),
@@ -315,7 +329,7 @@
             pltpu.VMEM((nh, own, depth), BF16),
             pltpu.VMEM((nh, own, depth), BF16),
             dma((5,)),
-            dma((groups, 3)),
+            dma((3,)),
             dma((nh,)),
             dma((nh,)),
             dma((nh,)),
@@ -326,7 +340,7 @@
             dma((chunks, nh)),
         ],
         compiler_params=pltpu.CompilerParams(
-            collective_id=0, has_side_effects=True, vmem_limit_bytes=60 * 2 ** 20),
+            collective_id=0, has_side_effects=True, vmem_limit_bytes=48 * 2 ** 20),
     )(tokens, w_qkv, lr_weight, lr_base, conv_weight, w_init, w_out)
 
 

time: 44.6 us -> 49.5 us (1.11)
  local copies, waits for them, and re-layouts: 1.54 us -> 7.29 us
  Pallas kernels: 42.7 us -> 41.9 us
    unnamed x1 -> x13, local copies, waits for them, and re-layouts: 1.54 us -> 7.29 us
    pallas_call x1, Pallas kernels: 42.7 us -> 41.9 us  [shards(): pl.pallas_call(functools.partial(layer, (n, nh, heads, hd, pair_group, ch...]
where the time goes in v2:
time: 49.5 us; the launch traced here: 49.2 us
  Pallas kernels  41.9 us (85%)
  local copies, waits for them, and re-layouts  7.29 us (15%)
    pallas_call x1, Pallas kernels, shards(): pl.pallas_call(functools.partial(layer, (n, nh, heads, hd, pair_group, ch...  41.9 us
    unnamed x13, local copies, waits for them, and re-layouts  7.29 us

profile of v2, /device:TPU:0, one launch (start us, length us, event | category | flops | bytes accessed | tf_op | source)
XLA Modules:
  0.0 49.2 jit_solution(6636702331176460602)
XLA Ops:
  0.0 0.0 copy-start
  0.0 2.3 %copy-done = bf16[768,3072]{1,0:T(8,128)(2,1)S(1)} copy-done((bf16[768,3072]{1,0:T(8,128)(2,1)S(1)}, bf16[768,3072]{1,0:T(8,128)(2,1)}, u32[]{:S(2)}) %copy-start) | copy-done | bytes 4718616
  2.3 0.0 copy-start.1
  2.3 1.1 %copy-done.1 = f32[2,12,64,64]{3,2,1,0:T(8,128)S(1)} copy-done((f32[2,12,64,64]{3,2,1,0:T(8,128)S(1)}, f32[2,12,64,64]{3,2,1,0:T(8,128)}, u32[]{:S(2)}) %copy-start.1) | copy-done | bytes 393240
  3.5 0.0 copy-start.2
  3.5 0.9 %copy-done.2 = bf16[16,3072]{1,0:T(8,128)(2,1)S(1)} copy-done((bf16[16,3072]{1,0:T(8,128)(2,1)S(1)}, bf16[16,3072]{1,0:T(8,128)(2,1)}, u32[]{:S(2)}) %copy-start.2) | copy-done | bytes 98328
  4.4 0.0 copy-start.3
  4.4 0.9 %copy-done.3 = bf16[12,3072]{1,0:T(8,128)(2,1)S(1)} copy-done((bf16[12,3072]{1,0:T(8,128)(2,1)S(1)}, bf16[12,3072]{1,0:T(8,128)(2,1)}, u32[]{:S(2)}) %copy-start.3) | copy-done | bytes 73752
  5.3 0.0 copy-start.4
  5.3 0.7 %copy-done.4 = f32[2,4,768]{2,1,0:T(4,128)S(1)} copy-done((f32[2,4,768]{2,1,0:T(4,128)S(1)}, f32[2,4,768]{2,1,0:T(4,128)}, u32[]{:S(2)}) %copy-start.4) | copy-done | bytes 24600
  6.0 0.0 copy-start.5
  6.0 0.7 %copy-done.5 = f32[12]{0:T(128)S(1)} copy-done((f32[12]{0:T(128)S(1)}, f32[12]{0:T(128)}, u32[]{:S(2)}) %copy-start.5) | copy-done | bytes 72
  6.7 41.9 %shard_map.73 = bf16[16,3072]{1,0:T(8,128)(2,1)S(1)} custom-call(bf16[16,3072]{1,0:T(8,128)(2,1)S(1)} %copy-done.2, bf16[3,768,3072]{2,1,0:T(8,128)(2,1)} %wqkv.1, bf16[12,3072]{1,0:T(8,128)(2,1)S(1)} %copy-done.3, f32[12]{0:T(128)S(1)} %copy-done.5, f32[2,4,768]{2,1,0:T(4,128)S(1)} %copy-done.4, f32[2,12,64,64]{3,2,1,0:T(8,128)S(1)} %copy-done.1, ...), custom_call_target="tpu_custom_call" | custom-call | tf_op jit(solution)/shard_map/pallas_call | solution.py:304
  48.6 0.6 %copy.9 = bf16[16,3072]{1,0:T(8,128)(2,1)} copy(bf16[16,3072]{1,0:T(8,128)(2,1)S(1)} %shard_map.73) | data formatting | bytes 196608
Async XLA Ops:
  0.0 2.3 %copy-start = (bf16[768,3072]{1,0:T(8,128)(2,1)S(1)}, bf16[768,3072]{1,0:T(8,128)(2,1)}, u32[]{:S(2)}) copy-start(bf16[768,3072]{1,0:T(8,128)(2,1)} %wout.1) | copy-start | bytes 14155780
  2.3 1.1 %copy-start.1 = (f32[2,12,64,64]{3,2,1,0:T(8,128)S(1)}, f32[2,12,64,64]{3,2,1,0:T(8,128)}, u32[]{:S(2)}) copy-start(f32[2,12,64,64]{3,2,1,0:T(8,128)} %winit.1) | copy-start | bytes 1179652
  3.5 0.9 %copy-start.2 = (bf16[16,3072]{1,0:T(8,128)(2,1)S(1)}, bf16[16,3072]{1,0:T(8,128)(2,1)}, u32[]{:S(2)}) copy-start(bf16[16,3072]{1,0:T(8,128)(2,1)} %tok.1) | copy-start | bytes 294916
  4.4 0.9 %copy-start.3 = (bf16[12,3072]{1,0:T(8,128)(2,1)S(1)}, bf16[12,3072]{1,0:T(8,128)(2,1)}, u32[]{:S(2)}) copy-start(bf16[12,3072]{1,0:T(8,128)(2,1)} %lrw.1) | copy-start | bytes 221188
  5.3 0.7 %copy-start.4 = (f32[2,4,768]{2,1,0:T(4,128)S(1)}, f32[2,4,768]{2,1,0:T(4,128)}, u32[]{:S(2)}) copy-start(f32[2,4,768]{2,1,0:T(4,128)} %cw.1) | copy-start | bytes 73732
  6.0 0.7 %copy-start.5 = (f32[12]{0:T(128)S(1)}, f32[12]{0:T(128)}, u32[]{:S(2)}) copy-start(f32[12]{0:T(128)} %lrb.1) | copy-start | bytes 148

commit v3 on v2

--- a/solution.py
+++ b/solution.py
@@ -25,8 +25,8 @@
 
 def layer(cfg, tok, wqkv, lrw, lrb, cw, winit, wout, out,
           xbuf, rim, halo, xs, xt, wv, wov, lrwv, cwv, cwt, taps_ref, wi, gate,
-          maps, adds, states, sending, reach, kept, pbuf, rbuf,
-          lsem, wsem, tsend, trecv, hsend, hrecv, rsend, rrecv, psend, precv):
+          maps, adds, states, sending, reach, kept, given, taken, pbuf, rbuf,
+          lsem, wsem, tsend, trecv, hsend, hrecv, gsend, grecv, rsend, rrecv, psend, precv):
     n, nh, heads, hd, pair_group, chunks = cfg
     own, depth = tok.shape
     rows = own * nh
@@ -36,6 +36,9 @@
     wide = 2 * hd
     g, me = lax.axis_index("seq"), lax.axis_index("head")
     not_first, not_last = g > 0, g < n - 1
+    core, chip, chips = lax.rem(g, 2), g // 2, n // 2
+    other = g + 1 - 2 * core
+    chip_before, chip_after = chip > 0, chip < chips - 1
     last_head = me == nh - 1
 
     small = [pltpu.make_async_copy(a, b, lsem.at[k]) for k, (a, b) in enumerate((
@@ -55,14 +58,20 @@
 
     @pl.when(not_first)
     def _():
-        pl.semaphore_signal(barrier, inc=1, device_id=(g - 1, me), device_id_type=MESH)
         pl.semaphore_signal(barrier, inc=1, device_id=(g - 1, nh - 1), device_id_type=MESH)
 
-    @pl.when(not_last)
-    def _():
-        pl.semaphore_signal(barrier, inc=1, device_id=(g + 1, me), device_id_type=MESH)
-
-    pl.semaphore_wait(barrier, (nh - 1) + jnp.where(not_first, 1, 0) + jnp.where(not_last, 1, 0)
+    pl.semaphore_signal(barrier, inc=1, device_id=(other, me), device_id_type=MESH)
+
+    @pl.when(chip_before)
+    def _():
+        pl.semaphore_signal(barrier, inc=1, device_id=(2 * chip - 1, me), device_id_type=MESH)
+
+    @pl.when(chip_after)
+    def _():
+        pl.semaphore_signal(barrier, inc=1, device_id=(2 * chip + 2, me), device_id_type=MESH)
+
+    relays_on = jnp.where(core == 1, chip_after, chip_before)
+    pl.semaphore_wait(barrier, nh + jnp.where(relays_on, 2, 0)
                       + jnp.where(last_head & not_last, nh, 0))
 
     def token_copy(i, slot):
@@ -104,7 +113,7 @@
     for j in range(pairs):
         taps_ref[pl.ds(j * LANES, LANES), :] = cwt[:, pl.ds(j * LANES, LANES)].T
 
-    for way, outer in ((0, jnp.logical_not(not_first)), (1, jnp.logical_not(not_last))):
+    for way, outer in ((0, jnp.logical_not(chip_before)), (1, jnp.logical_not(chip_after))):
         @pl.when(outer)
         def _():
             for p in range(pairs):
@@ -195,37 +204,66 @@
         made = [mm(lhs[j], rhs[j]) for j in each]
         for j in each:
             p = j
-            maps[way, p, :, pl.ds(0, wide)] = (-made[j][:wide, :wide]).astype(BF16)
+            step = (-made[j][:wide, :wide]).astype(BF16)
+            maps[way, p, :, pl.ds(0, wide)] = step
+            given[way, p, pl.ds(0, wide), :] = step
             maps[way, p, :, pl.ds(wide, wide)] = (q[j] - made[j][:wide, wide:]).astype(BF16)
-            adds[way, p] = made[j][wide:wide + hd] + made[j][wide + hd:]
-
-    def state_copy(way, gi):
+            shift = made[j][wide:wide + hd] + made[j][wide + hd:]
+            adds[way, p] = shift
+            given[way, p, pl.ds(wide, hd), :] = shift[:, :wide].astype(BF16)
+
+    def map_copy(gi):
         span = pl.ds(gi * pair_group, pair_group)
         return pltpu.make_async_remote_copy(
-            src_ref=sending.at[way, span], dst_ref=states.at[way, span],
-            send_sem=rsend.at[way, gi], recv_sem=rrecv.at[way, gi],
-            device_id=(g + 1 - 2 * way, me), device_id_type=MESH)
-
-    ways, normed = [], []
+            src_ref=given.at[core, span], dst_ref=taken.at[span],
+            send_sem=gsend.at[gi], recv_sem=grecv.at[gi],
+            device_id=(other, me), device_id_type=MESH)
+
+    for gi in range(groups):
+        map_copy(gi).start()
+    relay = 1 - core
+    for gi in range(groups):
+        map_copy(gi).wait_recv()
+        mine = range(gi * pair_group, (gi + 1) * pair_group)
+        first = [taken[p] for p in mine]
+        then = [mm(a, maps[relay, p]) for a, p in zip(first, mine)]
+        for a, b, p in zip(first, then, mine):
+            a = a.astype(F32)
+            near, far = pl.ds(0, wide), pl.ds(wide, wide)
+            maps[relay, p, :, near] = (maps[relay, p, :, near].astype(F32) + a[:wide]
+                                       + b[:wide, :wide]).astype(BF16)
+            maps[relay, p, :, far] = (maps[relay, p, :, far].astype(F32)
+                                      + b[:wide, wide:]).astype(BF16)
+            adds[relay, p, :, near] = adds[relay, p, :, near] + a[wide:] + b[wide:, :wide]
+            adds[relay, p, :, far] = adds[relay, p, :, far] + b[wide:, wide:]
+
+    def state_copy(way, gi, hop):
+        span = pl.ds(gi * pair_group, pair_group)
+        return pltpu.make_async_remote_copy(
+            src_ref=sending.at[span], dst_ref=states.at[way, span],
+            send_sem=rsend.at[gi, hop - 1], recv_sem=rrecv.at[way, gi],
+            device_id=(g + hop * (1 - 2 * way), me), device_id_type=MESH)
+
+    normed = []
     for d in range(2):
         way = jnp.where(g < n // 2, d, 1 - d)
-        starts = jnp.where(way == 0, g, n - 1 - g) == 0
-        ends = jnp.where(way == 0, n - 1 - g, g) == 0
-        ways.append((way, ends))
+        starts = jnp.where(way == 0, chip, chips - 1 - chip) == 0
+        onward = (way == relay) & relays_on
         for gi in range(groups):
             @pl.when(jnp.logical_not(starts))
             def _():
-                state_copy(way, gi).wait_recv()
+                state_copy(way, gi, 1).wait_recv()
 
             mine = range(gi * pair_group, (gi + 1) * pair_group)
             old = [states[way, p] for p in mine]
             new = [mm(a, maps[way, p]) + adds[way, p] for a, p in zip(old, mine)]
-            for a, b, p in zip(old, new, mine):
-                sending[way, p] = (a.astype(F32) + b[:, :wide]).astype(BF16)
-
-            @pl.when(jnp.logical_not(ends))
+
+            @pl.when(onward)
             def _():
-                state_copy(way, gi).start()
+                for a, b, p in zip(old, new, mine):
+                    sending[p] = (a.astype(F32) + b[:, :wide]).astype(BF16)
+                state_copy(way, gi, 2).start()
+                state_copy(way, gi, 1).start()
 
             for b, p in zip(new, mine):
                 reach[p] = b[:, wide:]
@@ -280,11 +318,14 @@
         for h in range(nh):
             halo_copy(h).wait_send()
 
-    for way, ends in ways:
-        @pl.when(jnp.logical_not(ends))
-        def _():
-            for gi in range(groups):
-                state_copy(way, gi).wait_send()
+    for gi in range(groups):
+        map_copy(gi).wait_send()
+
+    @pl.when(relays_on)
+    def _():
+        for gi in range(groups):
+            for hop in (1, 2):
+                state_copy(relay, gi, hop).wait_send()
 
 
 def shards(n, nh, tokens, w_qkv, lr_weight, lr_base, conv_weight, w_init, w_out):
@@ -323,9 +364,11 @@
             pltpu.VMEM((2, pairs, wide, 2 * wide), BF16),
             pltpu.VMEM((2, pairs, hd, 2 * wide), F32),
             pltpu.VMEM((2, pairs, hd, wide), BF16),
-            pltpu.VMEM((2, pairs, hd, wide), BF16),
+            pltpu.VMEM((pairs, hd, wide), BF16),
             pltpu.VMEM((pairs, hd, wide), F32),
             pltpu.VMEM((pairs, hd, wide), F32),
+            pltpu.VMEM((2, pairs, wide + hd, wide), BF16),
+            pltpu.VMEM((pairs, wide + hd, wide), BF16),
             pltpu.VMEM((nh, own, depth), BF16),
             pltpu.VMEM((nh, own, depth), BF16),
             dma((5,)),
@@ -334,13 +377,15 @@
             dma((nh,)),
             dma((nh,)),
             dma((1,)),
-            dma((2, groups)),
+            dma((groups,)),
+            dma((groups,)),
+            dma((groups, 2)),
             dma((2, groups)),
             dma((chunks, nh)),
             dma((chunks, nh)),
         ],
         compiler_params=pltpu.CompilerParams(
-            collective_id=0, has_side_effects=True, vmem_limit_bytes=48 * 2 ** 20),
+            collective_id=0, has_side_effects=True, vmem_limit_bytes=60 * 2 ** 20),
     )(tokens, w_qkv, lr_weight, lr_base, conv_weight, w_init, w_out)
 
 

time: 49.5 us -> 44.1 us (0.89)
  local copies, waits for them, and re-layouts: 7.29 us -> 1.54 us
  Pallas kernels: 41.9 us -> 42.4 us
    unnamed x13 -> x1, local copies, waits for them, and re-layouts: 7.29 us -> 1.54 us
where the time goes in v3:
time: 44.1 us; the launch traced here: 43.9 us
  Pallas kernels  42.4 us (96%)
  local copies, waits for them, and re-layouts  1.54 us (3%)
    pallas_call x1, Pallas kernels, shards(): pl.pallas_call(functools.partial(layer, (n, nh, heads, hd, pair_group, ch...  42.4 us
    unnamed x1, local copies, waits for them, and re-layouts  1.54 us

profile of v3, /device:TPU:0, one launch (start us, length us, event | category | flops | bytes accessed | tf_op | source)
XLA Modules:
  0.0 43.9 jit_solution(16002770180294686982)
XLA Ops:
  0.0 42.4 %shard_map.73 = bf16[16,3072]{1,0:T(8,128)(2,1)} custom-call(bf16[16,3072]{1,0:T(8,128)(2,1)} %tok.1, bf16[3,768,3072]{2,1,0:T(8,128)(2,1)} %wqkv.1, bf16[12,3072]{1,0:T(8,128)(2,1)} %lrw.1, f32[12]{0:T(128)} %lrb.1, f32[2,4,768]{2,1,0:T(4,128)} %cw.1, f32[2,12,64,64]{3,2,1,0:T(8,128)} %winit.1, bf16[768,3072]{1,0:T(8,128)(2,1)} %wout.1), custom_call_target="tpu_custom_call" | custom-call | tf_op jit(solution)/shard_map/pallas_call | solution.py:345
  42.4 1.5 %copy.9 = bf16[16,3072]{1,0:T(8,128)(2,1)} copy(bf16[16,3072]{1,0:T(8,128)(2,1)} %shard_map.73) | data formatting | bytes 196608

commit v4 on v3

--- a/solution.py
+++ b/solution.py
@@ -23,9 +23,9 @@
     return lax.dot_general(a, b, (((1,), (1,)), ((), ())), preferred_element_type=F32)
 
 
-def layer(cfg, tok, wqkv, lrw, lrb, cw, winit, wout, out,
+def layer(cfg, tok, wqkv, lrw, lrb, cw, winit, wout, shares,
           xbuf, rim, halo, xs, xt, wv, wov, lrwv, cwv, cwt, taps_ref, wi, gate,
-          maps, adds, states, sending, reach, kept, given, taken, pbuf, rbuf,
+          maps, adds, states, sending, reach, kept, given, taken, pbuf,
           lsem, wsem, tsend, trecv, hsend, hrecv, gsend, grecv, rsend, rrecv, psend, precv):
     n, nh, heads, hd, pair_group, chunks = cfg
     own, depth = tok.shape
@@ -50,7 +50,6 @@
         weights.append(pltpu.make_async_copy(wqkv.at[c], wv.at[c, pl.ds(0, inner)], wsem.at[c]))
         weights[c].start()
     out_weight = pltpu.make_async_copy(wout, wov, lsem.at[4])
-    out_weight.start()
 
     barrier = pltpu.get_barrier_semaphore()
     for i in range(1, nh):
@@ -62,16 +61,16 @@
 
     pl.semaphore_signal(barrier, inc=1, device_id=(other, me), device_id_type=MESH)
 
-    @pl.when(chip_before)
-    def _():
-        pl.semaphore_signal(barrier, inc=1, device_id=(2 * chip - 1, me), device_id_type=MESH)
-
-    @pl.when(chip_after)
-    def _():
-        pl.semaphore_signal(barrier, inc=1, device_id=(2 * chip + 2, me), device_id_type=MESH)
+    @pl.when(chip_before & (core == 1))
+    def _():
+        pl.semaphore_signal(barrier, inc=1, device_id=(2 * chip - 2 + core, me), device_id_type=MESH)
+
+    @pl.when(chip_after & (core == 0))
+    def _():
+        pl.semaphore_signal(barrier, inc=1, device_id=(2 * chip + 2 + core, me), device_id_type=MESH)
 
     relays_on = jnp.where(core == 1, chip_after, chip_before)
-    pl.semaphore_wait(barrier, nh + jnp.where(relays_on, 2, 0)
+    pl.semaphore_wait(barrier, nh + jnp.where(relays_on, 1, 0)
                       + jnp.where(last_head & not_last, nh, 0))
 
     def token_copy(i, slot):
@@ -178,6 +177,7 @@
         return total
 
     q_all, k_all, v_all = [convolved(c) for c in range(3)]
+    out_weight.start()
     each = range(pairs)
     part = [slice(j * wide, (j + 1) * wide) for j in each]
     root = [root_rate(j) for j in each]
@@ -237,12 +237,19 @@
             adds[relay, p, :, near] = adds[relay, p, :, near] + a[wide:] + b[wide:, :wide]
             adds[relay, p, :, far] = adds[relay, p, :, far] + b[wide:, wide:]
 
-    def state_copy(way, gi, hop):
+    def state_copy(way, gi):
         span = pl.ds(gi * pair_group, pair_group)
         return pltpu.make_async_remote_copy(
             src_ref=sending.at[span], dst_ref=states.at[way, span],
-            send_sem=rsend.at[gi, hop - 1], recv_sem=rrecv.at[way, gi],
-            device_id=(g + hop * (1 - 2 * way), me), device_id_type=MESH)
+            send_sem=rsend.at[gi, 0], recv_sem=rrecv.at[way, gi],
+            device_id=(g + 2 * (1 - 2 * way), me), device_id_type=MESH)
+
+    def leaf_copy(way, gi):
+        span = pl.ds(gi * pair_group, pair_group)
+        return pltpu.make_async_remote_copy(
+            src_ref=states.at[way, span], dst_ref=states.at[way, span],
+            send_sem=rsend.at[gi, 1], recv_sem=rrecv.at[way, gi],
+            device_id=(other, me), device_id_type=MESH)
 
     normed = []
     for d in range(2):
@@ -252,7 +259,7 @@
         for gi in range(groups):
             @pl.when(jnp.logical_not(starts))
             def _():
-                state_copy(way, gi, 1).wait_recv()
+                state_copy(way, gi).wait_recv()
 
             mine = range(gi * pair_group, (gi + 1) * pair_group)
             old = [states[way, p] for p in mine]
@@ -262,8 +269,11 @@
             def _():
                 for a, b, p in zip(old, new, mine):
                     sending[p] = (a.astype(F32) + b[:, :wide]).astype(BF16)
-                state_copy(way, gi, 2).start()
-                state_copy(way, gi, 1).start()
+                state_copy(way, gi).start()
+
+            @pl.when((way == relay) & jnp.logical_not(starts))
+            def _():
+                leaf_copy(way, gi).start()
 
             for b, p in zip(new, mine):
                 reach[p] = b[:, wide:]
@@ -287,7 +297,7 @@
     def share_copy(j, i, to, slot):
         cols = pl.ds(j * (depth // chunks), depth // chunks)
         return pltpu.make_async_remote_copy(
-            src_ref=pbuf.at[to, :, cols], dst_ref=rbuf.at[slot, :, cols],
+            src_ref=pbuf.at[to, :, cols], dst_ref=shares.at[slot, :, cols],
             send_sem=psend.at[j, i], recv_sem=precv.at[j, i],
             device_id=(g, to), device_id_type=MESH)
 
@@ -299,14 +309,12 @@
         for i in range(1, nh):
             share_copy(j, i, lax.rem(me + i, nh), me).start()
 
+    kept_share = pltpu.make_async_copy(pbuf.at[me], shares.at[me], lsem.at[0])
+    kept_share.start()
     for j in range(chunks):
-        cols = pl.ds(j * (depth // chunks), depth // chunks)
-        total = pbuf[me, :, cols].astype(F32)
         for i in range(1, nh):
-            sender = lax.rem(me + nh - i, nh)
-            share_copy(j, i, lax.rem(me + i, nh), sender).wait_recv()
-            total = total + rbuf[sender, :, cols].astype(F32)
-        out[:, cols] = total.astype(BF16)
+            share_copy(j, i, lax.rem(me + i, nh), lax.rem(me + nh - i, nh)).wait_recv()
+    kept_share.wait()
 
     for i in range(1, nh):
         token_copy(i, me).wait_send()
@@ -324,8 +332,12 @@
     @pl.when(relays_on)
     def _():
         for gi in range(groups):
-            for hop in (1, 2):
-                state_copy(relay, gi, hop).wait_send()
+            state_copy(relay, gi).wait_send()
+
+    @pl.when(jnp.where(core == 1, chip_before, chip_after))
+    def _():
+        for gi in range(groups):
+            leaf_copy(relay, gi).wait_send()
 
 
 def shards(n, nh, tokens, w_qkv, lr_weight, lr_base, conv_weight, w_init, w_out):
@@ -342,11 +354,11 @@
     hbm = pl.BlockSpec(memory_space=pltpu.HBM)
     smem = pl.BlockSpec(memory_space=pltpu.SMEM)
     dma = pltpu.SemaphoreType.DMA
-    return pl.pallas_call(
+    shares = pl.pallas_call(
         functools.partial(layer, (n, nh, heads, hd, pair_group, chunks)),
-        out_shape=jax.ShapeDtypeStruct((own, depth), BF16),
+        out_shape=jax.ShapeDtypeStruct((nh, own, depth), BF16),
         in_specs=[hbm, hbm, hbm, smem, hbm, hbm, hbm],
-        out_specs=pl.BlockSpec(memory_space=pltpu.VMEM),
+        out_specs=hbm,
         scratch_shapes=[
             pltpu.VMEM((nh, own, depth), BF16),
             pltpu.VMEM((16, depth // (KERNEL - 1)), BF16),
@@ -370,7 +382,6 @@
             pltpu.VMEM((2, pairs, wide + hd, wide), BF16),
             pltpu.VMEM((pairs, wide + hd, wide), BF16),
             pltpu.VMEM((nh, own, depth), BF16),
-            pltpu.VMEM((nh, own, depth), BF16),
             dma((5,)),
             dma((3,)),
             dma((nh,)),
@@ -387,6 +398,10 @@
         compiler_params=pltpu.CompilerParams(
             collective_id=0, has_side_effects=True, vmem_limit_bytes=60 * 2 ** 20),
     )(tokens, w_qkv, lr_weight, lr_base, conv_weight, w_init, w_out)
+    total = shares[0].astype(F32)
+    for p in range(1, nh):
+        total = total + shares[p].astype(F32)
+    return total.astype(BF16)
 
 
 def solution(mesh):

time: 44.1 us -> 43.4 us (0.984)
  other arithmetic: 0 us -> 1.73 us
  local copies, waits for them, and re-layouts: 1.54 us -> 0 us
  Pallas kernels: 42.4 us -> 41.5 us
    add x0 -> x1, other arithmetic: none -> 1.73 us  [shards(): total = total + shares[p].astype(F32)]
    unnamed x1 -> x0, local copies, waits for them, and re-layouts: 1.54 us -> none
    pallas_call x1, Pallas kernels: 42.4 us -> 41.5 us  [shards(): pl.pallas_call(functools.partial(layer, (n, nh, heads, hd, pair_group, ch...]
where the time goes in v4:
time: 43.4 us; the launch traced here: 43.2 us
  Pallas kernels  41.5 us (96%)
  other arithmetic  1.73 us (4%)
    pallas_call x1, Pallas kernels, shards(): pl.pallas_call(functools.partial(layer, (n, nh, heads, hd, pair_group, ch...  41.5 us
    add x1, other arithmetic, shards(): total = total + shares[p].astype(F32)  1.73 us

profile of v4, /device:TPU:0, one launch (start us, length us, event | category | flops | bytes accessed | tf_op | source)
XLA Modules:
  0.0 43.2 jit_solution(11248086860620140740)
XLA Ops:
  0.0 41.5 %shard_map.73 = bf16[4,16,3072]{2,1,0:T(8,128)(2,1)} custom-call(bf16[16,3072]{1,0:T(8,128)(2,1)} %tok.1, bf16[3,768,3072]{2,1,0:T(8,128)(2,1)} %wqkv.1, bf16[12,3072]{1,0:T(8,128)(2,1)} %lrw.1, f32[12]{0:T(128)} %lrb.1, f32[2,4,768]{2,1,0:T(4,128)} %cw.1, f32[2,12,64,64]{3,2,1,0:T(8,128)} %winit.1, bf16[768,3072]{1,0:T(8,128)(2,1)} %wout.1), custom_call_target="tpu_custom_call" | custom-call | tf_op jit(solution)/shard_map/pallas_call | solution.py:357
  41.5 1.7 %fusion = bf16[16,3072]{1,0:T(8,128)(2,1)} fusion(bf16[4,16,3072]{2,1,0:T(8,128)(2,1)} %shard_map.73), kind=kLoop, calls=%fused_computation.1 | loop fusion | flops 393216 | bytes 491520 | tf_op jit(solution)/shard_map/add | solution.py:403

commit v5 on v4

--- a/solution.py
+++ b/solution.py
@@ -24,7 +24,7 @@
 
 
 def layer(cfg, tok, wqkv, lrw, lrb, cw, winit, wout, shares,
-          xbuf, rim, halo, xs, xt, wv, wov, lrwv, cwv, cwt, taps_ref, wi, gate,
+          xbuf, rim, halo, xs, xt, wv, wov, lrwv, cwv, cwt, taps_ref, proj, wi, gate,
           maps, adds, states, sending, reach, kept, given, taken, pbuf,
           lsem, wsem, tsend, trecv, hsend, hrecv, gsend, grecv, rsend, rrecv, psend, precv):
     n, nh, heads, hd, pair_group, chunks = cfg
@@ -46,9 +46,14 @@
     for copy in small:
         copy.start()
     weights = []
-    for c in range(3):
-        weights.append(pltpu.make_async_copy(wqkv.at[c], wv.at[c, pl.ds(0, inner)], wsem.at[c]))
-        weights[c].start()
+    thirds = KERNEL - 1
+    piece = depth // thirds
+    for k in range(thirds):
+        cols = pl.ds(k * piece, piece)
+        weights.append([pltpu.make_async_copy(
+            wqkv.at[c, :, cols], wv.at[c, pl.ds(0, inner), cols], wsem.at[k, c]) for c in range(3)])
+        for copy in weights[k]:
+            copy.start()
     out_weight = pltpu.make_async_copy(wout, wov, lsem.at[4])
 
     barrier = pltpu.get_barrier_semaphore()
@@ -73,9 +78,11 @@
     pl.semaphore_wait(barrier, nh + jnp.where(relays_on, 1, 0)
                       + jnp.where(last_head & not_last, nh, 0))
 
-    def token_copy(i, slot):
-        return pltpu.make_async_remote_copy(
-            src_ref=tok, dst_ref=xbuf.at[slot], send_sem=tsend.at[i], recv_sem=trecv.at[i],
+    def token_copy(k, i, slot):
+        cols = pl.ds(k * piece, piece)
+        return pltpu.make_async_remote_copy(
+            src_ref=tok.at[:, cols], dst_ref=xbuf.at[slot, :, cols],
+            send_sem=tsend.at[k, i], recv_sem=trecv.at[k, i],
             device_id=(g, lax.rem(me + i, nh)), device_id_type=MESH)
 
     def halo_copy(h):
@@ -84,11 +91,10 @@
             device_id=(g + 1, h), device_id_type=MESH)
 
     for i in range(1, nh):
-        token_copy(i, me).start()
+        token_copy(0, i, me).start()
 
     small[0].wait()
     rim_rows = KERNEL - 1
-    piece = depth // rim_rows
     mine_last = xbuf[me].astype(F32)[own - rim_rows:]
     rim[...] = jnp.concatenate(
         [mine_last[r:r + 1, c * piece:(c + 1) * piece] for r in range(rim_rows) for c in range(rim_rows)]
@@ -99,6 +105,10 @@
         for h in range(nh):
             halo_copy(h).start()
 
+    for k in range(1, thirds):
+        for i in range(1, nh):
+            token_copy(k, i, me).start()
+
     @pl.when(jnp.logical_not(not_first))
     def _():
         halo[...] = jnp.zeros_like(halo)
@@ -110,7 +120,9 @@
     for c in range(2):
         cwt[pl.ds(c * KERNEL, KERNEL), pl.ds(0, inner)] = cwv[c]
     for j in range(pairs):
-        taps_ref[pl.ds(j * LANES, LANES), :] = cwt[:, pl.ds(j * LANES, LANES)].T
+        turned = cwt[:, pl.ds(j * LANES, LANES)].T
+        for p in range(2 * KERNEL):
+            taps_ref[p, pl.ds(j * LANES, LANES), :] = jnp.broadcast_to(turned[:, p:p + 1], (LANES, LANES))
 
     for way, outer in ((0, jnp.logical_not(chip_before)), (1, jnp.logical_not(chip_after))):
         @pl.when(outer)
@@ -119,28 +131,34 @@
                 second = wi[way, 2 * p + 1] if 2 * p + 1 < heads else jnp.zeros((hd, hd), F32)
                 states[way, p] = jnp.concatenate([wi[way, 2 * p], second], axis=1).astype(BF16)
 
-    for i in range(1, nh):
-        token_copy(i, lax.rem(me + nh - i, nh)).wait_recv()
-
     @pl.when(not_first)
     def _():
         halo_copy(0).wait_recv()
 
     tail = halo[...].astype(F32)
-    tail = [jnp.concatenate([tail[r * rim_rows + c:r * rim_rows + c + 1] for c in range(rim_rows)], axis=1)
-            for r in range(rim_rows)]
-    tail = jnp.concatenate([jnp.zeros((16 - rim_rows, depth), F32)] + tail, axis=0)
-    if own % 16 == 0:
-        for p in range(nh):
-            xt[pl.ds(p * own, own), :] = xbuf[p]
-    else:
-        for p in range(nh):
-            xs[pl.ds(p * own, own), :] = xbuf[p].astype(F32)
-        xt[pl.ds(0, rows), :] = xs[pl.ds(0, rows), :].astype(BF16)
-    xt[pl.ds(rows, LANES - 16 - rows), :] = jnp.zeros((LANES - 16 - rows, depth), BF16)
-    xt[pl.ds(LANES - 16, 16), :] = tail.astype(BF16)
-
-    gate[...] = jax.nn.sigmoid(mm_rows(lrwv[...], xt[...]))
+    logit = jnp.zeros((heads, LANES), F32)
+    for k in range(thirds):
+        cols = pl.ds(k * piece, piece)
+        for i in range(1, nh):
+            token_copy(k, i, lax.rem(me + nh - i, nh)).wait_recv()
+        if own % 16 == 0:
+            for p in range(nh):
+                xt[pl.ds(p * own, own), cols] = xbuf[p, :, cols]
+        else:
+            for p in range(nh):
+                xs[pl.ds(p * own, own), cols] = xbuf[p, :, cols].astype(F32)
+            xt[pl.ds(0, rows), cols] = xs[pl.ds(0, rows), cols].astype(BF16)
+        xt[pl.ds(rows, LANES - 16 - rows), cols] = jnp.zeros((LANES - 16 - rows, piece), BF16)
+        xt[pl.ds(LANES - 16, 16), cols] = jnp.concatenate(
+            [jnp.zeros((16 - rim_rows, piece), F32)]
+            + [tail[r * rim_rows + k:r * rim_rows + k + 1] for r in range(rim_rows)], axis=0).astype(BF16)
+        for c in range(3):
+            weights[k][c].wait()
+            share = mm_rows(wv[c, :, cols], xt[:, cols])
+            proj[c] = share if k == 0 else proj[c] + share
+        logit = logit + mm_rows(lrwv[:, cols], xt[:, cols])
+
+    gate[...] = jax.nn.sigmoid(logit)
 
     at_s = lax.broadcasted_iota(jnp.int32, (wide, wide), 0)
     at_t = lax.broadcasted_iota(jnp.int32, (wide, wide), 1)
@@ -162,18 +180,16 @@
         return jnp.sqrt(jnp.where(row_left, first, pltpu.roll(second, rows, 1)) / MB)
 
     def convolved(c):
-        weights[c].wait()
-        rounded = mm_rows(wv[c], xt[...]).astype(BF16).astype(F32)
+        rounded = proj[c].astype(BF16).astype(F32)
         if inner < pairs * wide:
             row = lax.broadcasted_iota(jnp.int32, rounded.shape, 0)
             rounded = jnp.where(row < inner, rounded, 0.0)
         if c == 2:
             return rounded
-        taps = taps_ref[...]
-        total = taps[:, c * KERNEL + KERNEL - 1:c * KERNEL + KERNEL] * rounded
+        total = taps_ref[c * KERNEL + KERNEL - 1] * rounded
         for p in range(KERNEL - 1):
             at = c * KERNEL + p
-            total = total + taps[:, at:at + 1] * pltpu.roll(rounded, KERNEL - 1 - p, 1)
+            total = total + taps_ref[at] * pltpu.roll(rounded, KERNEL - 1 - p, 1)
         return total
 
     q_all, k_all, v_all = [convolved(c) for c in range(3)]
@@ -317,7 +333,8 @@
     kept_share.wait()
 
     for i in range(1, nh):
-        token_copy(i, me).wait_send()
+        for k in range(thirds):
+            token_copy(k, i, me).wait_send()
         for j in range(chunks):
             share_copy(j, i, lax.rem(me + i, nh), me).wait_send()
 
@@ -370,7 +387,8 @@
             pltpu.VMEM(lr_weight.shape, BF16),
             pltpu.VMEM(conv_weight.shape, F32),
             pltpu.VMEM((LANES, padded), F32),
-            pltpu.VMEM((padded, LANES), F32),
+            pltpu.VMEM((2 * KERNEL, padded, LANES), F32),
+            pltpu.VMEM((3, padded, LANES), F32),
             pltpu.VMEM(w_init.shape, F32),
             pltpu.VMEM((heads, LANES), F32),
             pltpu.VMEM((2, pairs, wide, 2 * wide), BF16),
@@ -383,9 +401,9 @@
             pltpu.VMEM((pairs, wide + hd, wide), BF16),
             pltpu.VMEM((nh, own, depth), BF16),
             dma((5,)),
-            dma((3,)),
-            dma((nh,)),
-            dma((nh,)),
+            dma((KERNEL - 1, 3)),
+            dma((KERNEL - 1, nh)),
+            dma((KERNEL - 1, nh)),
             dma((nh,)),
             dma((1,)),
             dma((groups,)),

time: 43.4 us -> 43.3 us (level)
  no operation moved by 1% of the time
where the time goes in v5:
time: 43.3 us; the launch traced here: 43.1 us
  Pallas kernels  41.4 us (96%)
  other arithmetic  1.73 us (4%)
    pallas_call x1, Pallas kernels, shards(): pl.pallas_call(functools.partial(layer, (n, nh, heads, hd, pair_group, ch...  41.4 us
    add x1, other arithmetic, shards(): total = total + shares[p].astype(F32)  1.73 us

profile of v5, /device:TPU:0, one launch (start us, length us, event | category | flops | bytes accessed | tf_op | source)
XLA Modules:
  0.0 43.1 jit_solution(947641788671865045)
XLA Ops:
  0.0 41.4 %shard_map.73 = bf16[4,16,3072]{2,1,0:T(8,128)(2,1)} custom-call(bf16[16,3072]{1,0:T(8,128)(2,1)} %tok.1, bf16[3,768,3072]{2,1,0:T(8,128)(2,1)} %wqkv.1, bf16[12,3072]{1,0:T(8,128)(2,1)} %lrw.1, f32[12]{0:T(128)} %lrb.1, f32[2,4,768]{2,1,0:T(4,128)} %cw.1, f32[2,12,64,64]{3,2,1,0:T(8,128)} %winit.1, bf16[768,3072]{1,0:T(8,128)(2,1)} %wout.1), custom_call_target="tpu_custom_call" | custom-call | tf_op jit(solution)/shard_map/pallas_call | solution.py:374
  41.4 1.7 %fusion = bf16[16,3072]{1,0:T(8,128)(2,1)} fusion(bf16[4,16,3072]{2,1,0:T(8,128)(2,1)} %shard_map.73), kind=kLoop, calls=%fused_computation.1 | loop fusion | flops 393216 | bytes 491520 | tf_op jit(solution)/shard_map/add | solution.py:421

commit v6 on v5

--- a/solution.py
+++ b/solution.py
@@ -213,20 +213,7 @@
     inv = [eye - one[j] + two[j] - three[j] for j in each]
     both = [jnp.concatenate([a, a.T], axis=1).astype(BF16) for a in inv]
     kv = [mm(jnp.concatenate([kb[j], v[j]], axis=0), both[j]) for j in each]
-    for way, mask in ((0, causal), (1, anti)):
-        lhs = [a[:, way * wide:(way + 1) * wide].astype(BF16) for a in kv]
-        rhs = [jnp.concatenate(
-            [kt[j], jnp.where(mask, gram[j][:, wide:], 0.0).astype(BF16)], axis=1) for j in each]
-        made = [mm(lhs[j], rhs[j]) for j in each]
-        for j in each:
-            p = j
-            step = (-made[j][:wide, :wide]).astype(BF16)
-            maps[way, p, :, pl.ds(0, wide)] = step
-            given[way, p, pl.ds(0, wide), :] = step
-            maps[way, p, :, pl.ds(wide, wide)] = (q[j] - made[j][:wide, wide:]).astype(BF16)
-            shift = made[j][wide:wide + hd] + made[j][wide + hd:]
-            adds[way, p] = shift
-            given[way, p, pl.ds(wide, hd), :] = shift[:, :wide].astype(BF16)
+    lhs = [[a[:, way * wide:(way + 1) * wide].astype(BF16) for a in kv] for way in range(2)]
 
     def map_copy(gi):
         span = pl.ds(gi * pair_group, pair_group)
@@ -235,8 +222,26 @@
             send_sem=gsend.at[gi], recv_sem=grecv.at[gi],
             device_id=(other, me), device_id_type=MESH)
 
+    near, far = pl.ds(0, wide), pl.ds(wide, wide)
     for gi in range(groups):
+        for way in range(2):
+            for p in range(gi * pair_group, (gi + 1) * pair_group):
+                made = mm(lhs[way][p], kt[p])
+                step = (-made[:wide]).astype(BF16)
+                shift = made[wide:wide + hd] + made[wide + hd:]
+                maps[way, p, :, near] = step
+                adds[way, p, :, near] = shift
+                given[way, p, near, :] = step
+                given[way, p, pl.ds(wide, hd), :] = shift.astype(BF16)
         map_copy(gi).start()
+
+    for way, mask in ((0, causal), (1, anti)):
+        for p in each:
+            score = jnp.where(mask, gram[p][:, wide:], 0.0).astype(BF16)
+            made = mm(lhs[way][p], score)
+            maps[way, p, :, far] = (q[p] - made[:wide]).astype(BF16)
+            adds[way, p, :, far] = made[wide:wide + hd] + made[wide + hd:]
+
     relay = 1 - core
     for gi in range(groups):
         map_copy(gi).wait_recv()
@@ -245,7 +250,6 @@
         then = [mm(a, maps[relay, p]) for a, p in zip(first, mine)]
         for a, b, p in zip(first, then, mine):
             a = a.astype(F32)
-            near, far = pl.ds(0, wide), pl.ds(wide, wide)
             maps[relay, p, :, near] = (maps[relay, p, :, near].astype(F32) + a[:wide]
                                        + b[:wide, :wide]).astype(BF16)
             maps[relay, p, :, far] = (maps[relay, p, :, far].astype(F32)
@@ -277,6 +281,10 @@
             def _():
                 state_copy(way, gi).wait_recv()
 
+            @pl.when((way == relay) & jnp.logical_not(starts))
+            def _():
+                leaf_copy(way, gi).start()
+
             mine = range(gi * pair_group, (gi + 1) * pair_group)
             old = [states[way, p] for p in mine]
             new = [mm(a, maps[way, p]) + adds[way, p] for a, p in zip(old, mine)]
@@ -286,10 +294,6 @@
                 for a, b, p in zip(old, new, mine):
                     sending[p] = (a.astype(F32) + b[:, :wide]).astype(BF16)
                 state_copy(way, gi).start()
-
-            @pl.when((way == relay) & jnp.logical_not(starts))
-            def _():
-                leaf_copy(way, gi).start()
 
             for b, p in zip(new, mine):
                 reach[p] = b[:, wide:]
@@ -364,7 +368,7 @@
     rows = own * nh
     pairs = (heads + 1) // 2
     padded = pairs * 2 * hd
-    pair_group = 2 if pairs % 2 == 0 else 1
+    pair_group = max(k for k in (1, 2, 3) if pairs % k == 0)
     groups = pairs // pair_group
     chunks = 2
     wide = 2 * hd

time: 43.3 us -> 43.1 us (level)
  no operation moved by 1% of the time
where the time goes in v6:
time: 43.1 us; the launch traced here: 43 us
  Pallas kernels  41.3 us (96%)
  other arithmetic  1.73 us (4%)
    pallas_call x1, Pallas kernels, shards(): pl.pallas_call(functools.partial(layer, (n, nh, heads, hd, pair_group, ch...  41.3 us
    add x1, other arithmetic, shards(): total = total + shares[p].astype(F32)  1.73 us

profile of v6, /device:TPU:0, one launch (start us, length us, event | category | flops | bytes accessed | tf_op | source)
XLA Modules:
  0.0 43.0 jit_solution(5879516757759893344)
XLA Ops:
  0.0 41.3 %shard_map.73 = bf16[4,16,3072]{2,1,0:T(8,128)(2,1)} custom-call(bf16[16,3072]{1,0:T(8,128)(2,1)} %tok.1, bf16[3,768,3072]{2,1,0:T(8,128)(2,1)} %wqkv.1, bf16[12,3072]{1,0:T(8,128)(2,1)} %lrw.1, f32[12]{0:T(128)} %lrb.1, f32[2,4,768]{2,1,0:T(4,128)} %cw.1, f32[2,12,64,64]{3,2,1,0:T(8,128)} %winit.1, bf16[768,3072]{1,0:T(8,128)(2,1)} %wout.1), custom_call_target="tpu_custom_call" | custom-call | tf_op jit(solution)/shard_map/pallas_call | solution.py:378
  41.3 1.7 %fusion = bf16[16,3072]{1,0:T(8,128)(2,1)} fusion(bf16[4,16,3072]{2,1,0:T(8,128)(2,1)} %shard_map.73), kind=kLoop, calls=%fused_computation.1 | loop fusion | flops 393216 | bytes 491520 | tf_op jit(solution)/shard_map/add | solution.py:425
